TPU v7x, 32 devices: a whole 2x2x4 slice. The times are simulated.
32 devices in a mesh: dp: 8 (over z, x), fsdp: 4 (over y, core).
Axes of the slice: x: 2, y: 2, z: 4, core: 2. Of those that a mesh axis runs over, the one named last changes fastest.
Arguments:
- tokens: bfloat16 [16384, 1024], P(('dp', 'fsdp')), may hold values from -6 to 6
- segment: int32 [32, 512], P(('dp', 'fsdp')), may hold values from -1 to 5, as said below
- cotangent: bfloat16 [16384, 1024], P(('dp', 'fsdp')), may hold values from -6 to 6
- query_w: float32 [1024, 1024], P(('dp', 'fsdp')), may hold values from -0.1875 to 0.1875
- key_w: float32 [1024, 1024], P(('dp', 'fsdp')), may hold values from -0.1875 to 0.1875
- value_w: float32 [1024, 1024], P(('dp', 'fsdp')), may hold values from -0.1875 to 0.1875
- attn_out_w: float32 [1024, 1024], P(('dp', 'fsdp')), may hold values from -0.75 to 0.75
- up_w: float32 [1024, 4096], P(('dp', 'fsdp')), may hold values from -0.1875 to 0.1875
- down_w: float32 [4096, 1024], P(None, ('dp', 'fsdp')), may hold values from -0.09375 to 0.09375
- query_bias: float32 [1024], P(('dp', 'fsdp')), may hold values from -3 to 3
- value_bias: float32 [1024], P(('dp', 'fsdp')), may hold values from -2 to 2
- attn_out_bias: float32 [1024], P(('dp', 'fsdp')), may hold values from -2 to 2
- up_bias: float32 [4096], P(('dp', 'fsdp')), may hold values from -2 to 2
- down_bias: float32 [1024], P(('dp', 'fsdp')), may hold values from -2 to 2
- norm1_gain: float32 [1024], P(('dp', 'fsdp')), may hold values from 0.5 to 1.5
- norm1_shift: float32 [1024], P(('dp', 'fsdp')), may hold values from -2 to 2
- norm2_gain: float32 [1024], P(('dp', 'fsdp')), may hold values from 0.5 to 1.5
- norm2_shift: float32 [1024], P(('dp', 'fsdp')), may hold values from -2 to 2
Outputs:
- outputs: bfloat16 [16384, 1024], P(('dp', 'fsdp'))
- d_tokens: float32 [16384, 1024], P(('dp', 'fsdp'))
- d_query_w: float32 [1024, 1024], P(('dp', 'fsdp'))
- d_key_w: float32 [1024, 1024], P(('dp', 'fsdp'))
- d_value_w: float32 [1024, 1024], P(('dp', 'fsdp'))
- d_attn_out_w: float32 [1024, 1024], P(('dp', 'fsdp'))
- d_up_w: float32 [1024, 4096], P(('dp', 'fsdp'))
- d_down_w: float32 [4096, 1024], P(None, ('dp', 'fsdp'))
- d_query_bias: float32 [1024], P(('dp', 'fsdp'))
- d_value_bias: float32 [1024], P(('dp', 'fsdp'))
- d_attn_out_bias: float32 [1024], P(('dp', 'fsdp'))
- d_up_bias: float32 [4096], P(('dp', 'fsdp'))
- d_down_bias: float32 [1024], P(('dp', 'fsdp'))
- d_norm1_gain: float32 [1024], P(('dp', 'fsdp'))
- d_norm1_shift: float32 [1024], P(('dp', 'fsdp'))
- d_norm2_gain: float32 [1024], P(('dp', 'fsdp'))
- d_norm2_shift: float32 [1024], P(('dp', 'fsdp'))
Inputs may be any that keep to these rules, and one draw needn't show every extreme that they name: `segment`: within each row, ids start at 0 and never fall over its real tokens; padding tokens hold -1 and stand only at a row's end; every row has real tokens.
All inputs are finite; a program needn't handle non-finite values.
Results may differ from a plain program's by a relative error of at most 0.02.
Values may be sent and summed in bfloat16 or wider, within the bound.
A program may use at most 192 MiB of HBM per device.

v0:
```python
import functools

import jax
import jax.numpy as jnp
from jax import lax
from jax.experimental import pallas as pl
from jax.experimental.pallas import tpu as pltpu
from jax.sharding import PartitionSpec as P

MESH = pl.DeviceIdType.MESH
BLOCKS = 12
DP, FSDP = BOTH = ("dp", "fsdp")


class Place:
    def __init__(self):
        dp, fs = lax.axis_index(DP), lax.axis_index(FSDP)
        z, x, y, c = self.z, self.x, self.y, self.c = dp // 2, dp % 2, fs // 2, fs % 2
        self.fs = fs
        self.near = z + 1 - 2 * (z % 2)
        self.other = 3 - z
        self.low = 2 * (z // 2)
        self.high = 2 - self.low
        self.near_pair, self.far_pair = pl.ds(self.low, 2), pl.ds(self.high, 2)
        self.far_one = z // 2 * -1 + 2
        self.far_two = 3 - z // 2 * 3
        self.inside = (z == 1) | (z == 2)
        self.to_x, self.to_y = device(z, 1 - x, y, c), device(z, x, 1 - y, c)
        self.to_c = device(z, x, y, 1 - c)
        self.to_near, self.to_other = device(self.near, x, y, c), device(self.other, x, y, c)


def device(z, x, y, c):
    return (z * 2 + x, y * 2 + c)


def greet(at):
    bar = pltpu.get_barrier_semaphore()

    def hail(peer):
        pl.semaphore_signal(bar, inc=1, device_id=peer, device_id_type=MESH)

    def meet(*peers):
        for peer in peers:
            hail(peer)
        pl.semaphore_wait(bar, len(peers))

    always = (at.to_c, at.to_x, at.to_y, at.to_near)
    pl.when(at.inside)(lambda: meet(*always, at.to_other))
    pl.when(jnp.logical_not(at.inside))(lambda: meet(*always))


def send(src, dst, ssem, rsem, peer):
    return pltpu.make_async_remote_copy(
        src_ref=src, dst_ref=dst, send_sem=ssem, recv_sem=rsem, device_id=peer, device_id_type=MESH
    )


def numbered(*names):
    return {name: i for i, name in enumerate(names)}


GATHER_GETS = numbered(
    "near", "one", "two", "xn", "yn", "xf", "yf", "da", "db", "df", "xo", "yo",
    "c0", "c1", "c2", "c3", "c4", "c5", "c6", "c7",
)


C_NAMES = list(GATHER_GETS)[-8:]


class GatherBlock:
    def __init__(self, at, full, mine, ss, rs, early=False):
        self.at, self.full, self.mine, self.ss, self.rs, self.early = at, full, mine, ss, rs, early

    def piece(self, name):
        a, full = self.at, self.full
        x, y, c = a.x, a.y, a.c
        both = {"n": a.near_pair, "f": a.far_pair}
        return {
            "own": lambda: full.at[a.z, x, y, c],
            "near": lambda: full.at[a.near, x, y, c],
            "one": lambda: full.at[a.far_one, x, y, c],
            "two": lambda: full.at[a.far_two, x, y, c],
            "on": lambda: full.at[both["n"], x, y, c],
            "of": lambda: full.at[both["f"], x, y, c],
            "xn": lambda: full.at[both["n"], 1 - x, y, c],
            "xf": lambda: full.at[both["f"], 1 - x, y, c],
            "yn": lambda: full.at[both["n"], x, 1 - y, c],
            "yf": lambda: full.at[both["f"], x, 1 - y, c],
            "dn": lambda: full.at[both["n"], 1 - x, 1 - y, c],
            "df": lambda: full.at[both["f"], 1 - x, 1 - y, c],
            "xo": lambda: full.at[a.z, 1 - x, y, c],
            "yo": lambda: full.at[a.z, x, 1 - y, c],
            "x_near": lambda: full.at[a.near, 1 - x, y, c],
            "x_own": lambda: full.at[a.z, 1 - x, y, c],
            "y_near": lambda: full.at[a.near, x, 1 - y, c],
            "d_own": lambda: full.at[a.z, 1 - x, 1 - y, c],
            "d_near": lambda: full.at[a.near, 1 - x, 1 - y, c],
            "c0": lambda: full.at[both["n"], x, y, 1 - c],
            "c1": lambda: full.at[both["f"], x, y, 1 - c],
            "c2": lambda: full.at[both["n"], 1 - x, y, 1 - c],
            "c3": lambda: full.at[both["n"], x, 1 - y, 1 - c],
            "c4": lambda: full.at[both["n"], 1 - x, 1 - y, 1 - c],
            "c5": lambda: full.at[both["f"], 1 - x, y, 1 - c],
            "c6": lambda: full.at[both["f"], x, 1 - y, 1 - c],
            "c7": lambda: full.at[both["f"], 1 - x, 1 - y, 1 - c],
        }[name]()

    SENDS = {
        "own_near": ("own", "near", "to_near"),
        "own_other": ("own", "one", "to_other"),
        "near_other": ("near", "two", "to_other"),
        "one_near": ("one", "one", "to_near"),
        "two_near": ("two", "two", "to_near"),
        "xn": ("on", "xn", "to_x"),
        "yn": ("on", "yn", "to_y"),
        "xo": ("own", "xo", "to_x"),
        "yo": ("own", "yo", "to_y"),
        "xp": ("near", "xn", "to_x"),
        "yp": ("near", "yn", "to_y"),
        "xf": ("of", "xf", "to_x"),
        "yf": ("of", "yf", "to_y"),
        "da": ("x_own", "da", "to_y"),
        "db": ("y_near", "db", "to_x"),
        "d_other": ("dn", "df", "to_other"),
        "d_near": ("df", "df", "to_near"),
        "c0": ("on", "c0", "to_c"),
        "c1": ("of", "c1", "to_c"),
        "c2": ("xn", "c2", "to_c"),
        "c3": ("yn", "c3", "to_c"),
        "c4": ("dn", "c4", "to_c"),
        "c5": ("xf", "c5", "to_c"),
        "c6": ("yf", "c6", "to_c"),
        "c7": ("df", "c7", "to_c"),
    }
    ARRIVES = {"da": "d_own", "db": "d_near"}
    INSIDE = ("own_other", "near_other", "one_near", "two_near", "d_other", "d_near")

    def move(self, name):
        what, called, whom = self.SENDS[name]
        piece = self.piece(what)
        return send(
            piece, piece, self.ss.at[list(self.SENDS).index(name)], self.rs.at[GATHER_GETS[called]], getattr(self.at, whom)
        )

    def go(self, *names):
        for name in names:
            if name in self.INSIDE:
                pl.when(self.at.inside)(lambda: self.move(name).start())
            else:
                self.move(name).start()

    def get(self, name, what=None):
        piece = self.piece(what or self.ARRIVES.get(name, name))
        send(piece, piece, self.ss.at[0], self.rs.at[GATHER_GETS[name]], self.at.to_c).wait_recv()

    def stage(self, s):
        a = self.at
        if s == 0:
            self.full[a.z, a.x, a.y, a.c] = self.mine()
            self.go("own_near", "own_other")
            if self.early:
                self.go("xo", "yo")
        if s == 1:
            self.get("near")
            self.go("near_other")
            if self.early:
                self.go("xp", "yp", "c0")
            else:
                self.go("xn", "yn", "c0")
        if s == 2:
            self.get("one")
            self.go("one_near")
        if s == 3:
            self.get("two")
            self.go("two_near", "xf", "yf", "c1")
        if s == 4:
            if self.early:
                self.get("xo")
                self.go("da")
                self.get("xn", "x_near")
                self.go("c2")
                self.get("yo")
                self.get("yn", "y_near")
            else:
                self.get("xn")
                self.go("da", "c2")
                self.get("yn")
            self.go("db", "c3")
        if s == 5:
            self.get("da")
            self.get("db")
            self.go("d_other", "c4")
        if s == 6:
            self.get("xf")
            self.go("c5")
            self.get("yf")
            self.go("c6")
        if s == 7:
            self.get("df")
            self.go("d_near", "c7")
        if s == 8:
            for i in range(8):
                self.get(C_NAMES[i])
        if s == 9:
            for name in self.SENDS:
                if name not in self.INSIDE + (("xn", "yn") if self.early else ("xo", "yo", "xp", "yp")):
                    self.move(name).wait_send()

            @pl.when(a.inside)
            def _():
                for name in self.INSIDE:
                    self.move(name).wait_send()


GATHER_LAGS = (0, 1, 3, 6, 6, 7, 8, 8, 9, 11)
GATHER_ORDER = (4, 3, 5, 1, 0, 2, 6, 8, 7, 9)


HEAD = 64


norm_epsilon = 1e-12
masked_score = -1000000000.0


def to_half(array):
    return array.astype(jnp.bfloat16)


def matmul(left, right):
    return jnp.dot(left, right, preferred_element_type=jnp.float32)


def matmul_nt(left, right):
    return lax.dot_general(
        left, right, (((1,), (1,)), ((), ())), preferred_element_type=jnp.float32
    )


def contract_rows(left, right):
    return lax.dot_general(
        left, right, (((0,), (0,)), ((), ())), preferred_element_type=jnp.float32
    )


def column_sums(array):
    return jnp.sum(array.astype(jnp.float32), axis=0)


def normalize(values, gain_vec, shift_vec):
    center = values - jnp.mean(values, axis=-1, keepdims=True)
    spread = jnp.mean(center * center, axis=-1, keepdims=True)
    return center * lax.rsqrt(spread + norm_epsilon) * gain_vec + shift_vec


def gelu_exact(values):
    return jax.nn.gelu(values, approximate=False)


def split_heads(block):
    return block.reshape(block.shape[0], -1, HEAD)


def row_scores(queries, key_rows, labels):
    scores = (
        jnp.einsum("qhe,khe->hqk", queries, key_rows, preferred_element_type=jnp.float32) * 0.125
    )
    allowed = labels[:, None] == labels[None, :]
    return jnp.where(allowed[None], scores, masked_score)


def attend_row(pieces):
    queries, key_rows, value_rows, labels = pieces
    scores = row_scores(split_heads(queries), split_heads(key_rows), labels)
    row_max = jnp.max(scores, axis=-1, keepdims=True)
    row_exp = jnp.exp(scores - row_max)
    row_total = jnp.sum(row_exp, axis=-1, keepdims=True)
    probs_half = to_half(row_exp / row_total)
    context = jnp.einsum(
        "hqk,khe->qhe", probs_half, split_heads(value_rows), preferred_element_type=jnp.float32
    )
    return (to_half(context.reshape(queries.shape)), (row_max + jnp.log(row_total))[..., 0])


def attend_back(pieces):
    queries, key_rows, value_rows, labels, log_total, d_context = pieces
    query_heads = split_heads(queries)
    key_heads = split_heads(key_rows)
    context_heads = split_heads(d_context)
    scores = row_scores(query_heads, key_heads, labels)
    attn_probs = jnp.exp(scores - log_total[..., None])
    d_probs = jnp.einsum(
        "qhe,khe->hqk", context_heads, split_heads(value_rows), preferred_element_type=jnp.float32
    )
    row_delta = jnp.sum(attn_probs * d_probs, axis=-1, keepdims=True)
    d_scores = to_half(attn_probs * (d_probs - row_delta))
    d_queries = (
        jnp.einsum("hqk,khe->qhe", d_scores, key_heads, preferred_element_type=jnp.float32) * 0.125
    )
    d_keys = (
        jnp.einsum("hqk,qhe->khe", d_scores, query_heads, preferred_element_type=jnp.float32)
        * 0.125
    )
    d_values = jnp.einsum(
        "hqk,qhe->khe", to_half(attn_probs), context_heads, preferred_element_type=jnp.float32
    )
    return (
        to_half(d_queries.reshape(queries.shape)),
        to_half(d_keys.reshape(queries.shape)),
        to_half(d_values.reshape(queries.shape)),
    )


def plain_device(
    tokens,
    segment,
    cotangent,
    query_w,
    key_w,
    value_w,
    attn_out_w,
    up_w,
    down_w,
    query_bias,
    value_bias,
    attn_out_bias,
    up_bias,
    down_bias,
    norm1_gain,
    norm1_shift,
    norm2_gain,
    norm2_shift,
):
    row_count = segment.shape[0]
    row_length = segment.shape[1]
    model_width = tokens.shape[1]

    def by_rows(array):
        return array.reshape(row_count, row_length, -1)

    attn_set = (
        lax.all_gather(to_half(query_w), BOTH, axis=0, tiled=True),
        lax.all_gather(to_half(key_w), BOTH, axis=0, tiled=True),
        lax.all_gather(to_half(value_w), BOTH, axis=0, tiled=True),
        lax.all_gather(to_half(attn_out_w), BOTH, axis=0, tiled=True),
        lax.all_gather(to_half(query_bias), BOTH, axis=0, tiled=True),
        lax.all_gather(to_half(value_bias), BOTH, axis=0, tiled=True),
        lax.all_gather(to_half(attn_out_bias), BOTH, axis=0, tiled=True),
        lax.all_gather(to_half(norm1_gain), BOTH, axis=0, tiled=True),
        lax.all_gather(to_half(norm1_shift), BOTH, axis=0, tiled=True),
    )
    wq_full, wk_full, wv_full, wo_full, bias_q, bias_v, bias_o, gain_one, shift_one = attn_set
    ffn_set = (
        lax.all_gather(to_half(up_w), BOTH, axis=0, tiled=True),
        lax.all_gather(to_half(down_w), BOTH, axis=1, tiled=True),
        lax.all_gather(to_half(up_bias), BOTH, axis=0, tiled=True),
        lax.all_gather(to_half(down_bias), BOTH, axis=0, tiled=True),
        lax.all_gather(to_half(norm2_gain), BOTH, axis=0, tiled=True),
        lax.all_gather(to_half(norm2_shift), BOTH, axis=0, tiled=True),
    )
    w_up, w_down, bias_up, bias_down, gain_two, shift_two = ffn_set
    queries = to_half(matmul(tokens, wq_full) + bias_q.astype(jnp.float32))
    key_rows = to_half(matmul(tokens, wk_full))
    value_rows = to_half(matmul(tokens, wv_full) + bias_v.astype(jnp.float32))
    context, log_total = lax.map(
        attend_row, (by_rows(queries), by_rows(key_rows), by_rows(value_rows), segment)
    )
    context = context.reshape(-1, model_width)
    attended = matmul(context, wo_full) + bias_o.astype(jnp.float32)
    first_sum = tokens.astype(jnp.float32) + attended
    norm_mid, pull_one = jax.vjp(
        normalize, first_sum, gain_one.astype(jnp.float32), shift_one.astype(jnp.float32)
    )
    mid_half = to_half(norm_mid)
    pre_act = matmul(mid_half, w_up) + bias_up.astype(jnp.float32)
    act_out, pull_act = jax.vjp(gelu_exact, pre_act)
    act_half = to_half(act_out)
    ffn_out = matmul(act_half, w_down) + bias_down.astype(jnp.float32)
    second_sum = mid_half.astype(jnp.float32) + ffn_out
    final, pull_two = jax.vjp(
        normalize, second_sum, gain_two.astype(jnp.float32), shift_two.astype(jnp.float32)
    )
    outputs = to_half(final)
    valid = (segment.reshape(-1) >= 0).astype(jnp.float32)[:, None]
    d_out = cotangent.astype(jnp.float32) * valid
    d_second, d_gain_two, d_shift_two = pull_two(d_out)
    up_back, down_back = (
        lax.all_gather(to_half(up_w), BOTH, axis=0, tiled=True),
        lax.all_gather(to_half(down_w), BOTH, axis=1, tiled=True),
    )
    d_ffn = to_half(d_second)
    d_down_turned = contract_rows(d_ffn, act_half)
    d_down_bias = column_sums(d_ffn)
    (d_pre,) = pull_act(matmul_nt(d_ffn, down_back))
    d_pre_half = to_half(d_pre)
    d_up_w = contract_rows(mid_half, d_pre_half)
    d_up_bias = column_sums(d_pre_half)
    d_mid = d_second + matmul_nt(d_pre_half, up_back)
    d_first, d_gain_one, d_shift_one = pull_one(d_mid)
    wq_back, wk_back, wv_back, wo_back = (
        lax.all_gather(to_half(query_w), BOTH, axis=0, tiled=True),
        lax.all_gather(to_half(key_w), BOTH, axis=0, tiled=True),
        lax.all_gather(to_half(value_w), BOTH, axis=0, tiled=True),
        lax.all_gather(to_half(attn_out_w), BOTH, axis=0, tiled=True),
    )
    d_att = to_half(d_first)
    d_attn_out_w = contract_rows(context, d_att)
    d_attn_out_bias = column_sums(d_att)
    d_context = to_half(matmul_nt(d_att, wo_back))
    d_queries, d_keys, d_values = lax.map(
        attend_back,
        (
            by_rows(queries),
            by_rows(key_rows),
            by_rows(value_rows),
            segment,
            log_total,
            by_rows(d_context),
        ),
    )
    d_queries = d_queries.reshape(-1, model_width)
    d_keys = d_keys.reshape(-1, model_width)
    d_values = d_values.reshape(-1, model_width)
    d_query_w = contract_rows(tokens, d_queries)
    d_key_w = contract_rows(tokens, d_keys)
    d_value_w = contract_rows(tokens, d_values)
    d_query_bias = column_sums(d_queries)
    d_value_bias = column_sums(d_values)
    d_tokens = (
        d_first
        + matmul_nt(d_queries, wq_back)
        + matmul_nt(d_keys, wk_back)
        + matmul_nt(d_values, wv_back)
    )
    members = (
        d_query_w,
        d_key_w,
        d_value_w,
        d_attn_out_w,
        d_up_w,
        d_down_turned,
        d_query_bias,
        d_value_bias,
        d_attn_out_bias,
        d_up_bias,
        d_down_bias,
        d_gain_one,
        d_shift_one,
        d_gain_two,
        d_shift_two,
    )
    block_sums = (
        lax.psum_scatter(
            members[0].astype(jnp.bfloat16), DP, scatter_dimension=0, tiled=True
        ).astype(jnp.float32),
        lax.psum_scatter(
            members[1].astype(jnp.bfloat16), DP, scatter_dimension=0, tiled=True
        ).astype(jnp.float32),
        lax.psum_scatter(
            members[2].astype(jnp.bfloat16), DP, scatter_dimension=0, tiled=True
        ).astype(jnp.float32),
        lax.psum_scatter(
            members[3].astype(jnp.bfloat16), DP, scatter_dimension=0, tiled=True
        ).astype(jnp.float32),
        lax.psum_scatter(
            members[4].astype(jnp.bfloat16), DP, scatter_dimension=0, tiled=True
        ).astype(jnp.float32),
        lax.psum_scatter(
            members[5].astype(jnp.bfloat16), DP, scatter_dimension=0, tiled=True
        ).astype(jnp.float32),
        lax.psum_scatter(
            members[6].astype(jnp.bfloat16), DP, scatter_dimension=0, tiled=True
        ).astype(jnp.float32),
        lax.psum_scatter(
            members[7].astype(jnp.bfloat16), DP, scatter_dimension=0, tiled=True
        ).astype(jnp.float32),
        lax.psum_scatter(
            members[8].astype(jnp.bfloat16), DP, scatter_dimension=0, tiled=True
        ).astype(jnp.float32),
        lax.psum_scatter(
            members[9].astype(jnp.bfloat16), DP, scatter_dimension=0, tiled=True
        ).astype(jnp.float32),
        lax.psum_scatter(
            members[10].astype(jnp.bfloat16), DP, scatter_dimension=0, tiled=True
        ).astype(jnp.float32),
        lax.psum_scatter(
            members[11].astype(jnp.bfloat16), DP, scatter_dimension=0, tiled=True
        ).astype(jnp.float32),
        lax.psum_scatter(
            members[12].astype(jnp.bfloat16), DP, scatter_dimension=0, tiled=True
        ).astype(jnp.float32),
        lax.psum_scatter(
            members[13].astype(jnp.bfloat16), DP, scatter_dimension=0, tiled=True
        ).astype(jnp.float32),
        lax.psum_scatter(
            members[14].astype(jnp.bfloat16), DP, scatter_dimension=0, tiled=True
        ).astype(jnp.float32),
    )
    every_shard = (
        lax.psum_scatter(
            block_sums[0].astype(jnp.bfloat16), FSDP, scatter_dimension=0, tiled=True
        ).astype(jnp.float32),
        lax.psum_scatter(
            block_sums[1].astype(jnp.bfloat16), FSDP, scatter_dimension=0, tiled=True
        ).astype(jnp.float32),
        lax.psum_scatter(
            block_sums[2].astype(jnp.bfloat16), FSDP, scatter_dimension=0, tiled=True
        ).astype(jnp.float32),
        lax.psum_scatter(
            block_sums[3].astype(jnp.bfloat16), FSDP, scatter_dimension=0, tiled=True
        ).astype(jnp.float32),
        lax.psum_scatter(
            block_sums[4].astype(jnp.bfloat16), FSDP, scatter_dimension=0, tiled=True
        ).astype(jnp.float32),
        lax.psum_scatter(
            block_sums[5].astype(jnp.bfloat16), FSDP, scatter_dimension=0, tiled=True
        ).astype(jnp.float32),
        lax.psum_scatter(
            block_sums[6].astype(jnp.bfloat16), FSDP, scatter_dimension=0, tiled=True
        ).astype(jnp.float32),
        lax.psum_scatter(
            block_sums[7].astype(jnp.bfloat16), FSDP, scatter_dimension=0, tiled=True
        ).astype(jnp.float32),
        lax.psum_scatter(
            block_sums[8].astype(jnp.bfloat16), FSDP, scatter_dimension=0, tiled=True
        ).astype(jnp.float32),
        lax.psum_scatter(
            block_sums[9].astype(jnp.bfloat16), FSDP, scatter_dimension=0, tiled=True
        ).astype(jnp.float32),
        lax.psum_scatter(
            block_sums[10].astype(jnp.bfloat16), FSDP, scatter_dimension=0, tiled=True
        ).astype(jnp.float32),
        lax.psum_scatter(
            block_sums[11].astype(jnp.bfloat16), FSDP, scatter_dimension=0, tiled=True
        ).astype(jnp.float32),
        lax.psum_scatter(
            block_sums[12].astype(jnp.bfloat16), FSDP, scatter_dimension=0, tiled=True
        ).astype(jnp.float32),
        lax.psum_scatter(
            block_sums[13].astype(jnp.bfloat16), FSDP, scatter_dimension=0, tiled=True
        ).astype(jnp.float32),
        lax.psum_scatter(
            block_sums[14].astype(jnp.bfloat16), FSDP, scatter_dimension=0, tiled=True
        ).astype(jnp.float32),
    )
    (
        shard_qw,
        shard_kw,
        shard_vw,
        shard_ow,
        shard_uw,
        shard_turned,
        shard_qb,
        shard_vb,
        shard_ob,
        shard_ub,
        shard_db,
        shard_g1,
        shard_s1,
        shard_g2,
        shard_s2,
    ) = every_shard
    shard_dw = jnp.transpose(shard_turned)
    return (
        outputs,
        d_tokens,
        shard_qw,
        shard_kw,
        shard_vw,
        shard_ow,
        shard_uw,
        shard_dw,
        shard_qb,
        shard_vb,
        shard_ob,
        shard_ub,
        shard_db,
        shard_g1,
        shard_s1,
        shard_g2,
        shard_s2,
    )


ATTN = 4
LANES = 128
SIDE = 1024
V_LANE, R_LANE = 32, 64


def aligned(start, size, step=None):
    return pl.ds(pl.multiple_of(start, step or size), size)


def side_loop(count, body):
    def step(i, carry):
        body(i)
        return carry

    lax.fori_loop(0, count, step, 0)


def square(full, b):
    size = full.shape[-1]
    return full.at[b].reshape(size, size)


def spread_vectors(tiles, short_ref, up_ref, depth):
    for dp in range(2 * depth):
        total = jnp.zeros((16, LANES), jnp.float32)
        for fs in range(4):
            total = total + tiles[dp // 2, dp % 2, fs // 2, fs % 2].astype(jnp.float32)
        short_ref[:, dp * LANES : (dp + 1) * LANES] = total[:8]
        for fs in range(4):
            at = (dp * 4 + fs) * LANES
            up_ref[:, at : at + LANES] = total[8 + fs : 9 + fs]


def stepwise(body, after):
    def step(i):
        body(i)
        for k, follow in enumerate(after):
            pl.when(i == k)(follow)

    side_loop(len(after), step)


def nothing():
    pass


def attend_pairs(first, last, qkvc, lse, mask):
    length = mask.shape[0]

    def pair(p):
        lanes = aligned(p * LANES, LANES)
        q, k, v = qkvc[0, :, lanes], qkvc[1, :, lanes], qkvc[2, :, lanes]
        lane = lax.broadcasted_iota(jnp.int32, (length, LANES), 1)
        lower = lane < HEAD
        total = jnp.zeros((length, LANES), jnp.float32)
        logs = lse[...]
        for h in range(2):
            here = lower if h == 0 else jnp.logical_not(lower)
            key = jnp.where(here, k, jnp.zeros_like(k))
            scores = matmul_nt(q, key) + mask[...]
            row_max = jnp.max(scores, axis=-1, keepdims=True)
            row_exp = jnp.exp(scores - row_max)
            row_total = jnp.sum(row_exp, axis=-1, keepdims=True)
            part = matmul(to_half(row_exp), v) / row_total
            total = jnp.where(here, part, total)
            logs = jnp.where(lane == 2 * p + h, row_max + jnp.log(row_total), logs)
        qkvc[3, :, lanes] = to_half(total)
        lse[...] = logs

    def step(i, carry):
        pair(i)
        return carry

    lax.fori_loop(first, last, step, 0)


SUM_SENDS = numbered("c", "df", "dg", "da", "db", "xn", "yn", "xf", "yf", "f", "m", "n")
SUM_LAGS = (0, 1, 2, 3, 4, 3, 5, 6, 7)
SUM_ORDER = (1, 6, 4, 2, 7, 3, 0, 5, 8)
SUM_BUFFERS = {
    "grad": (2, (4, 2, 2, 2)),
    "held": (7, (4, 2, 2)),
    "c": (2, (4, 2, 2)),
    "df": (7, (2,)),
    "dg": (4, (2,)),
    "da": (2, ()),
    "db": (2, ()),
    "xn": (4, (2,)),
    "yn": (3, (2,)),
    "xf": (5, (2,)),
    "yf": (5, (2,)),
    "f": (5, (2,)),
    "m": (4, (2,)),
    "n": (4, ()),
}


def sum_scratch(rows, cols, blocks, names):
    bufs = [SUM_BUFFERS[name] for name in names]
    bufs = [pltpu.VMEM((min(slots, blocks),) + parts + (rows, cols), jnp.bfloat16) for slots, parts in bufs]
    return bufs + [pltpu.SemaphoreType.DMA((blocks, len(SUM_SENDS)))] * 2


class SumBlock:
    def __init__(self, at, refs, names, b, **others):
        self.at = at
        *bufs, ss, rs = refs
        self.ss, self.rs = ss.at[b], rs.at[b]
        self.buf = {n: ref.at[b % ref.shape[0]] for n, ref in zip(names, bufs)} | others

    def move(self, name):
        a, held = self.at, self.buf["held"]
        x, y = a.x, a.y
        every, both = pl.ds(0, 4), pl.ds(0, 2)
        src, to = {
            "c": lambda: (self.buf["grad"].at[every, both, both, 1 - a.c], a.to_c),
            "df": lambda: (held.at[a.far_pair, 1 - x, 1 - y], a.to_near),
            "dg": lambda: (held.at[a.far_pair, 1 - x, 1 - y], a.to_other),
            "da": lambda: (held.at[a.z, 1 - x, 1 - y], a.to_y),
            "db": lambda: (held.at[a.near, 1 - x, 1 - y], a.to_x),
            "xn": lambda: (held.at[a.near_pair, 1 - x, y], a.to_x),
            "yn": lambda: (held.at[a.near_pair, x, 1 - y], a.to_y),
            "xf": lambda: (held.at[a.far_pair, 1 - x, y], a.to_x),
            "yf": lambda: (held.at[a.far_pair, x, 1 - y], a.to_y),
            "f": lambda: (held.at[a.far_pair, x, y], a.to_near),
            "m": lambda: (held.at[a.far_pair, x, y], a.to_other),
            "n": lambda: (held.at[a.near, x, y], a.to_near),
        }[name]()
        i = SUM_SENDS[name]
        return send(src, self.buf[name], self.ss.at[i], self.rs.at[i], to)

    def start(self, name):
        self.move(name).start()

    def got(self, name):
        self.move(name).wait_recv()
        return self.buf[name]

    def stage(self, s, out=None):
        a, held, grad = self.at, self.buf["held"], self.buf["grad"]
        x, y, c = a.x, a.y, a.c
        inside = a.inside
        outside = jnp.logical_not(inside)

        def add(first, xx, yy, *others, count=2):
            for i in range(count):
                total = held[first + i, xx, yy].astype(jnp.float32)
                for other in others:
                    total = total + (other[i] if count == 2 else other[...]).astype(jnp.float32)
                held[first + i, xx, yy] = total.astype(jnp.bfloat16)

        if s == 0:
            self.start("c")
        if s == 1:
            self.move("c").wait()
            pair = self.buf["c"]

            def join(first, xx, yy):
                for i in range(2):
                    held[first + i, xx, yy] = grad[first + i, xx, yy, c] + pair[first + i, xx, yy]

            join(a.high, 1 - x, 1 - y)
            pl.when(outside)(lambda: self.start("df"))
            join(a.high, 1 - x, y)
            self.start("xf")
            join(a.high, x, 1 - y)
            self.start("yf")
            join(a.low, 1 - x, 1 - y)
            join(a.low, 1 - x, y)
            join(a.low, x, 1 - y)
            join(a.high, x, y)
            join(a.low, x, y)
        if s == 2:

            @pl.when(inside)
            def _():
                add(a.high, 1 - x, 1 - y, self.got("df"))
                self.start("dg")

        if s == 3:

            @pl.when(inside)
            def _():
                add(a.low, 1 - x, 1 - y, self.got("dg"))

            self.start("da")
            self.start("db")
        if s == 4:
            add(a.z, 1 - x, y, self.got("da"), count=1)
            self.start("xn")
            add(a.near, x, 1 - y, self.got("db"), count=1)
            self.start("yn")
        if s == 5:
            add(a.high, x, y, self.got("xf"), self.got("yf"))
            pl.when(outside)(lambda: self.start("f"))
        if s == 6:

            @pl.when(inside)
            def _():
                add(a.high, x, y, self.got("f"))
                self.start("m")

        if s == 7:
            add(a.low, x, y, self.got("xn"), self.got("yn"))

            @pl.when(inside)
            def _():
                add(a.low, x, y, self.got("m"))

            self.start("n")
        if s == 8:
            out[...] = held[a.z, x, y].astype(jnp.float32) + self.got("n")[...].astype(jnp.float32)
            for name in ("da", "db", "xn", "yn", "xf", "yf", "n"):
                self.move(name).wait_send()

            @pl.when(inside)
            def _():
                self.move("dg").wait_send()
                self.move("m").wait_send()

            @pl.when(outside)
            def _():
                self.move("df").wait_send()
                self.move("f").wait_send()


def attend_back_pairs(first, last, qkvc, lse, delta, mask, grads):
    length = mask.shape[0]

    def pair(p, carry):
        lanes = aligned(p * LANES, LANES)
        q, k, v, d_context = qkvc[0, :, lanes], qkvc[1, :, lanes], qkvc[2, :, lanes], grads[3, :, lanes]
        lower = lax.broadcasted_iota(jnp.int32, (length, LANES), 1) < HEAD
        sums = [jnp.zeros((length, LANES), jnp.float32) for _ in range(3)]
        for h in range(2):
            here = lower if h == 0 else jnp.logical_not(lower)
            row = pl.ds(2 * p + h, 1)
            key = jnp.where(here, k, jnp.zeros_like(k))
            value = jnp.where(here, v, jnp.zeros_like(v))
            probs = jnp.exp(matmul_nt(key, q) + mask[...] - lse[row, :])
            d_scores = to_half(probs * (matmul_nt(value, d_context) - delta[row, :]))
            parts = (
                contract_rows(d_scores, k) * 0.125,
                matmul(d_scores, q),
                matmul(to_half(probs), d_context),
            )
            sums = [jnp.where(here, part, total) for part, total in zip(parts, sums)]
        for i in range(3):
            grads[i, :, lanes] = to_half(sums[i])
        return carry

    lax.fori_loop(first, last, pair, 0)


SUM_NAMES = tuple(SUM_BUFFERS)
LENT = SUM_NAMES[:2]
OWN_BUFFERS = SUM_NAMES[2:]


def layer_kernel(depth, *refs):
    tokens_hbm, segment, cotangent_hbm, wq, wk, wv, wo, up_w, down_w, *vectors = refs[:18]
    out_hbm, dtok_hbm, gq, gk, gv, go, gup, gdown, gshort, gup_bias = refs[18:28]
    (
        full, tiles, mine_vec, short, up_bias, qkvc, lse, lse_turned, mask, mid, act, dge, nhat, total, half,
        turn_a, delta_turned, cotangent, vgrads, tile_sum, spare, staged, ss, rs, isem, osem, *rest,
    ) = refs[28:]
    count = len(OWN_BUFFERS) + 2
    big, vec = rest[:count], rest[count:]
    length, width = mid.shape
    tokens = mid
    here = Place()
    fs = here.fs
    rows = wq.shape[0]
    f32 = jnp.float32

    shards = [wq, wk, wv, wo]
    for wide in (up_w, down_w):
        shards += [wide.at[:, i * width : (i + 1) * width] for i in range(ATTN)]
    loads = [
        pltpu.make_async_copy(src, total.at[i * rows : (i + 1) * rows], isem.at[i]) for i, src in enumerate(shards)
    ]
    loads.append(pltpu.make_async_copy(tokens_hbm, tokens, isem.at[BLOCKS]))
    loads.append(pltpu.make_async_copy(cotangent_hbm, cotangent, isem.at[BLOCKS + 1]))
    for load in loads:
        load.start()
    greet(here)

    mine_vec[...] = jnp.zeros_like(mine_vec)
    for i in range(8):
        mine_vec[i : i + 1, 0:rows] = vectors[i][...]
    placed = pltpu.roll(mine_vec[...], fs * rows, 1)
    row_at = lax.broadcasted_iota(jnp.int32, (16, LANES), 0)
    mine_vec[...] = jnp.where(row_at == 8 + fs, jnp.broadcast_to(vectors[8][...], (16, LANES)), placed)

    def own(b):
        loads[b].wait()
        return to_half(total[b * rows : (b + 1) * rows, :])

    def gather_block(b):
        return GatherBlock(here, full.at[b], lambda: own(b), ss.at[b], rs.at[b], b < 2)

    own_tiles = GatherBlock(here, tiles, lambda: to_half(mine_vec[...]), ss.at[BLOCKS], rs.at[BLOCKS])

    def gather_pump(t):
        for s in GATHER_ORDER:
            b = t - GATHER_LAGS[s]
            if 0 <= b < BLOCKS:
                gather_block(b).stage(s)
            if b == 0:
                own_tiles.stage(s)

    gather_pump(0)
    gather_pump(1)
    labels = segment[...].astype(jnp.float32)
    turned = jnp.transpose(jnp.broadcast_to(labels, (LANES, length)))
    mask[...] = jnp.where(turned[:, :1] == labels, 0.0, masked_score)
    lse[...] = jnp.where(turned >= 0.0, 1.0, 0.0)
    for t in range(2, 10):
        gather_pump(t)
    spread_vectors(tiles, short, up_bias, depth)
    loads[BLOCKS].wait()

    def project(i):
        biased = jnp.where(i == 1, 0.0, 1.0)
        scale = jnp.where(i == 0, 0.125, 1.0)
        bias = short[pl.ds(i // 2, 1), :] * biased
        qkvc[i] = to_half(to_half(matmul(tokens[...], square(full, i)[...]) + bias).astype(f32) * scale)

    stepwise(project, [lambda: gather_pump(10), lambda: gather_pump(11), nothing])
    stepwise(
        lambda i: attend_pairs(i * 4, i * 4 + 4, qkvc, lse, mask),
        [lambda: gather_pump(12), nothing],
    )
    lse_turned[...] = jnp.transpose(lse[...])[: lse_turned.shape[0]]
    gather_pump(13)

    wo_full = square(full, 3)

    def attended(n):
        cols = aligned(n * SIDE, SIDE)
        total[:, cols] = (
            matmul(qkvc[3], wo_full[:, cols]) + short[2:3, cols] + tokens[:, cols].astype(jnp.float32)
        )

    side_loop(width // SIDE, attended)

    lane_at = lax.broadcasted_iota(jnp.int32, (LANES, LANES), 1)

    def first_norm(i):
        at = aligned(i * LANES, LANES)
        values = total[at, :]
        center = values - jnp.mean(values, axis=-1, keepdims=True)
        spread = jnp.mean(center * center, axis=-1, keepdims=True)
        r = lax.rsqrt(spread + norm_epsilon)
        unit = center * r
        nhat[at, :] = to_half(unit)
        lse[at, :] = jnp.where(lane_at >= R_LANE, r, lse[at, :])
        mid[at, :] = to_half(unit * short[4:5, :] + short[5:6, :])

    side_loop(length // LANES, first_norm)

    def activate(j):
        weight = square(full, ATTN + j)
        for part in range(2):
            cols = slice(part * width // 2, (part + 1) * width // 2)
            pre = matmul(mid[...], weight[:, cols]) + up_bias[:, aligned(j * width + part * width // 2, width // 2)]
            cdf = 0.5 * (1.0 + lax.erf(pre * 0.7071067811865476))
            act[j, :, cols] = to_half(pre * cdf)
            pdf = jnp.exp(-0.5 * pre * pre) * 0.3989422804014327
            dge[j, :, cols] = to_half(cdf + pre * pdf)

    def contract(j):
        total[...] = total[...] + matmul_nt(act[j], square(full, 2 * ATTN + j)[...])

    gather_pump(14)
    stepwise(activate, [lambda: gather_pump(15), lambda: gather_pump(16), lambda: gather_pump(17), nothing])
    total[...] = mid[...].astype(f32) + short[3:4, :]
    stepwise(contract, [lambda: gather_pump(18), lambda: gather_pump(19), lambda: gather_pump(20), nothing])

    loads[BLOCKS + 1].wait()
    vgrads[...] = jnp.zeros_like(vgrads)

    def second_norm(i):
        at = aligned(i * LANES, LANES)
        values = total[at, :]
        center = values - jnp.mean(values, axis=-1, keepdims=True)
        spread = jnp.mean(center * center, axis=-1, keepdims=True)
        r = lax.rsqrt(spread + norm_epsilon)
        unit = center * r
        gain = short[6:7, :]
        final = to_half(unit * gain + short[7:8, :])
        e = cotangent[at, :].astype(jnp.float32) * lse[at, V_LANE : V_LANE + 1]
        cotangent[at, :] = final
        vgrads[6:7, :] = vgrads[6:7, :] + jnp.sum(e * unit, axis=0, keepdims=True)
        vgrads[7:8, :] = vgrads[7:8, :] + jnp.sum(e, axis=0, keepdims=True)
        eg = e * gain
        d = r * (
            eg - jnp.mean(eg, axis=-1, keepdims=True) - unit * jnp.mean(eg * unit, axis=-1, keepdims=True)
        )
        total[at, :] = d
        half[at, :] = to_half(d)
        vgrads[3:4, :] = vgrads[3:4, :] + jnp.sum(to_half(d).astype(jnp.float32), axis=0, keepdims=True)

    side_loop(length // LANES, second_norm)
    pltpu.make_async_copy(cotangent, out_hbm, osem.at[0]).start()

    outs = [gdown.at[:, i * width : (i + 1) * width] for i in range(4)]
    outs += [gup.at[:, i * width : (i + 1) * width] for i in range(4)] + [go, gv, gk, gq]

    held_at = [(4, 0), (4, 1), (9, 0), (9, 1), (5, 0), (5, 1), (10, 0)]

    def grad_of(b):
        return spare.at[b % 2]

    def block(b):
        gathered, half_at = held_at[b % len(held_at)]
        lent = dict(zip(LENT, (grad_of(b), full.at[gathered, :, :, :, half_at])))
        return SumBlock(here, big, OWN_BUFFERS, b, **lent)

    vblock = SumBlock(here, vec, SUM_NAMES, 0)
    turn_b = square(full, 6).at[:, 0:length]

    def leave(b):
        return pltpu.make_async_copy(staged.at[b % 2], outs[b], osem.at[2 + b % 2])

    def pump(t):
        for s in SUM_ORDER:
            b = t - SUM_LAGS[s]
            if 0 <= b < BLOCKS:
                if s == 8 and b > 1:
                    leave(b - 2).wait()
                block(b).stage(s, staged.at[b % 2])
                if s == 8:
                    leave(b).start()
            if b == BLOCKS - 1:
                vblock.stage(s, tile_sum)

    def weight_grad(b, left, right):
        grad = grad_of(b)
        for part in range(2):
            got = to_half(matmul(left[part * width // 2 : (part + 1) * width // 2, :], right[...]))
            grad[2 * part : 2 * part + 2] = got.reshape((2,) + grad.shape[1:])

    def sums_of(values):
        return jnp.sum(values.astype(f32), axis=0, keepdims=True)

    turn_a[...] = jnp.transpose(half[...])
    weight_grad(0, turn_a, act.at[0])
    pump(0)
    for t in range(21, BLOCKS + max(GATHER_LAGS)):
        gather_pump(t)

    up_grads = up_bias

    def units_back(j):
        d_pre = to_half(matmul(half[...], square(full, 2 * ATTN + j)[...]) * dge[j].astype(f32))
        dge[j] = d_pre
        up_grads[:, aligned(j * width, width)] = sums_of(d_pre)
        add_product(dge.at[j], square(full, ATTN + j))

        @pl.when(j < ATTN - 1)
        def _():
            weight_grad(j + 1, turn_a, act.at[j + 1])

    def add_product(left, weight):
        total[...] = total[...] + matmul_nt(left[...], weight[...])

    stepwise(units_back, [lambda: pump(1), lambda: pump(2), lambda: pump(3), nothing])
    turn_b[...] = jnp.transpose(mid[...])
    loads[BLOCKS].start()
    weight_grad(4, turn_b, dge.at[0])
    pump(4)


    def first_norm_back(i):
        at = aligned(i * LANES, LANES)
        e = total[at, :]
        unit = nhat[at, :].astype(f32)
        vgrads[4:5, :] = vgrads[4:5, :] + jnp.sum(e * unit, axis=0, keepdims=True)
        vgrads[5:6, :] = vgrads[5:6, :] + jnp.sum(e, axis=0, keepdims=True)
        eg = e * short[4:5, :]
        d = lse[at, R_LANE : R_LANE + 1] * (
            eg - jnp.mean(eg, axis=-1, keepdims=True) - unit * jnp.mean(eg * unit, axis=-1, keepdims=True)
        )
        total[at, :] = d
        d_half = to_half(d)
        half[at, :] = d_half
        vgrads[2:3, :] = vgrads[2:3, :] + jnp.sum(d_half.astype(f32), axis=0, keepdims=True)

    side_loop(length // LANES, first_norm_back)
    wo_full = square(full, 3)
    delta = lse

    def context_back(n):
        cols = aligned(n * SIDE, SIDE)
        d_context = to_half(matmul_nt(half[...], wo_full[cols, :]))
        act[3, :, cols] = d_context
        product = d_context.astype(f32) * qkvc[3, :, cols].astype(f32)
        lane = lax.broadcasted_iota(jnp.int32, (length, LANES), 1)
        got = delta[...]
        for i in range(SIDE // HEAD):
            two = product[:, (i // 2) * LANES : (i // 2 + 1) * LANES]
            here = lane // HEAD == i % 2
            head = jnp.sum(jnp.where(here, two, 0.0), axis=-1, keepdims=True)
            got = jnp.where(lane == n * (SIDE // HEAD) + i, head, got)
        delta[...] = got

    side_loop(width // SIDE, context_back)
    delta_turned[...] = jnp.transpose(delta[...])[: delta_turned.shape[0]]
    weight_grad(5, turn_b, dge.at[1])
    pump(5)

    def attention_step(i):
        attend_back_pairs(3 * i, jnp.minimum(3 * i + 3, 8), qkvc, lse_turned, delta_turned, mask, act)

        @pl.when(i < 2)
        def _():
            weight_grad(6 + i, turn_b, dge.at[2 + i])

    stepwise(attention_step, [lambda: pump(6), lambda: pump(7), nothing])
    turn_a[...] = jnp.transpose(qkvc[3])
    weight_grad(8, turn_a, half)
    pump(8)
    loads[BLOCKS].wait()
    turn_b[...] = jnp.transpose(tokens[...])

    def place_vectors():
        vgrads[0:1, :] = sums_of(act[0])
        vgrads[1:2, :] = sums_of(act[2])
        for dp in range(2 * depth):
            for fsdp in range(4):
                at = (dp * 4 + fsdp) * LANES
                vec[0][0, dp // 2, dp % 2, fsdp // 2, fsdp % 2] = to_half(
                    jnp.concatenate(
                        [
                            vgrads[:, dp * LANES : (dp + 1) * LANES],
                            jnp.broadcast_to(up_grads[:, at : at + LANES], (8, LANES)),
                        ],
                        axis=0,
                    )
                )

    def last_pump():
        place_vectors()
        pump(11)

    stepwise(
        lambda i: weight_grad(9 + i, turn_b, act.at[2 - i]), [lambda: pump(9), lambda: pump(10), last_pump]
    )

    def hand_back():
        pltpu.make_async_copy(total, dtok_hbm, osem.at[1]).start()
        pump(14)

    stepwise(
        lambda i: add_product(act.at[2 - i], square(full, 2 - i)), [lambda: pump(12), lambda: pump(13), hand_back]
    )
    for t in range(15, BLOCKS + max(SUM_LAGS)):
        pump(t)
    leave(BLOCKS - 2).wait()
    leave(BLOCKS - 1).wait()
    moved = pltpu.roll(tile_sum[...], (4 - fs) * rows % LANES, 1)
    gshort[...] = moved[:8]
    gup_bias[...] = tile_sum[8:9, :]
    pltpu.make_async_copy(total, dtok_hbm, osem.at[1]).wait()
    pltpu.make_async_copy(cotangent, out_hbm, osem.at[0]).wait()


def layer_call(depth, tokens, segment, cotangent, weights, vectors):
    length, width = tokens.shape
    rows = weights[0].shape[0]
    dims = (depth, 2, 2, 2)
    bf, f32 = jnp.bfloat16, jnp.float32
    part = ((rows, width), f32)
    shapes = [
        ((length, width), bf), ((length, width), f32), part, part, part, part, ((rows, ATTN * width), f32),
        ((rows, ATTN * width), f32), ((8, LANES), f32), ((1, LANES), f32),
    ]
    vmem, hbm = pl.BlockSpec(memory_space=pltpu.VMEM), pl.BlockSpec(memory_space=pl.ANY)
    scratch = [
        pltpu.VMEM((BLOCKS,) + dims + (rows, width), bf),
        pltpu.VMEM(dims + (16, LANES), bf),
        pltpu.VMEM((16, LANES), f32),
        pltpu.VMEM((8, width), f32),
        pltpu.VMEM((1, ATTN * width), f32),
        pltpu.VMEM((4, length, width), bf),
        pltpu.VMEM((length, LANES), f32),
        pltpu.VMEM((width // HEAD, length), f32),
        pltpu.VMEM((length, length), f32),
        pltpu.VMEM((length, width), bf),
        pltpu.VMEM((ATTN, length, width), bf),
        pltpu.VMEM((ATTN, length, width), bf),
        pltpu.VMEM((length, width), bf),
        pltpu.VMEM((length, width), f32),
        pltpu.VMEM((length, width), bf),
        pltpu.VMEM((width, length), bf),
        pltpu.VMEM((width // HEAD, length), f32),
        pltpu.VMEM((length, width), bf),
        pltpu.VMEM((8, width), f32),
        pltpu.VMEM((16, LANES), f32),
        pltpu.VMEM((2,) + dims + (rows, width), bf),
        pltpu.VMEM((2, rows, width), f32),
        pltpu.SemaphoreType.DMA((BLOCKS + 1, len(GatherBlock.SENDS))),
        pltpu.SemaphoreType.DMA((BLOCKS + 1, len(GATHER_GETS))),
        pltpu.SemaphoreType.DMA((BLOCKS + 2,)),
        pltpu.SemaphoreType.DMA((4,)),
    ]
    scratch += sum_scratch(rows, width, BLOCKS, OWN_BUFFERS) + sum_scratch(16, LANES, 1, SUM_NAMES)
    return pl.pallas_call(
        functools.partial(layer_kernel, depth),
        out_shape=tuple(jax.ShapeDtypeStruct(*s) for s in shapes),
        in_specs=[hbm, vmem, hbm] + [hbm] * 6 + [vmem] * 9,
        out_specs=tuple([hbm] * 8 + [vmem] * 2),
        scratch_shapes=scratch,
        compiler_params=pltpu.CompilerParams(
            collective_id=0, has_side_effects=True, vmem_limit_bytes=63 * 2**20
        ),
        name="layer",
    )(tokens, segment, cotangent, *weights, *vectors)


PIECE = 1024


def results_kernel(large, short, *refs):
    sources, targets, vectors = refs[:large], refs[large + 2 : 2 * large + 2], refs[2 * large + 2 : 2 * large + 11]
    rows, up = refs[large : large + 2]
    held, (came, gone) = refs[2 * large + 11 : -2], refs[-2:]
    ins, outs = [], []
    for src, mid, dst in zip(sources, held, targets):
        for start in range(0, src.shape[0], PIECE):
            at = pl.ds(start, min(PIECE, src.shape[0]))
            i = len(ins)
            ins.append(pltpu.make_async_copy(src.at[at], mid.at[at], came.at[i]))
            outs.append(pltpu.make_async_copy(mid.at[at], dst.at[at], gone.at[i]))
    for copy in ins:
        copy.start()
    for i in range(8):
        vectors[i][...] = rows[i : i + 1, 0:short]
    vectors[8][...] = up[...]
    for copy, onward in zip(ins, outs):
        copy.wait()
        onward.start()
    for copy in outs:
        copy.wait()


def results_call(large, rows, up, short):
    vmem, hbm = pl.BlockSpec(memory_space=pltpu.VMEM), pl.BlockSpec(memory_space=pl.ANY)
    shapes = [jax.ShapeDtypeStruct(a.shape, a.dtype) for a in large]
    shapes += [jax.ShapeDtypeStruct((1, short), jnp.float32)] * 8 + [jax.ShapeDtypeStruct(up.shape, jnp.float32)]
    return pl.pallas_call(
        functools.partial(results_kernel, len(large), short),
        out_shape=tuple(shapes),
        in_specs=[hbm] * len(large) + [vmem] * 2,
        out_specs=tuple([hbm] * len(large) + [vmem] * 9),
        scratch_shapes=[pltpu.VMEM(a.shape, a.dtype) for a in large]
        + [pltpu.SemaphoreType.DMA((sum(-(-a.shape[0] // PIECE) for a in large),))] * 2,
        name="results",
    )(*large, rows, up)


def kernel_device(
    tokens, segment, cotangent, query_w, key_w, value_w, attn_out_w, up_w, down_w, query_bias, value_bias,
    attn_out_bias, up_bias, down_bias, norm1_gain, norm1_shift, norm2_gain, norm2_shift,
):
    depth = lax.axis_size(DP) // 2
    weights = (query_w, key_w, value_w, attn_out_w, up_w, jnp.transpose(down_w))
    vectors = (
        query_bias, value_bias, attn_out_bias, down_bias, norm1_gain, norm1_shift, norm2_gain, norm2_shift, up_bias,
    )
    outputs, d_tokens, qw, kw, vw, ow, uw, dw, short_sum, up_sum = layer_call(
        depth, tokens, segment, cotangent, weights, [vector[None] for vector in vectors]
    )
    outputs, d_tokens, qw, kw, vw, ow, uw, dw, *vectors = results_call(
        (outputs, d_tokens, qw, kw, vw, ow, uw, dw), short_sum, up_sum, query_w.shape[0]
    )
    qb, vb, ob, db, g1, s1, g2, s2, ub = [vector.reshape(-1) for vector in vectors]
    return (
        outputs, d_tokens, qw, kw, vw, ow, uw, jnp.transpose(dw), qb, vb, ob, ub, db, g1, s1, g2, s2,
    )


def solution(mesh):
    fits = mesh.shape[FSDP] == 4 and mesh.shape[DP] == 8
    body = kernel_device if fits else plain_device
    in_specs = (
        P(BOTH, None),
        P(BOTH, None),
        P(BOTH, None),
        P(BOTH, None),
        P(BOTH, None),
        P(BOTH, None),
        P(BOTH, None),
        P(BOTH, None),
        P(None, BOTH),
        P(BOTH),
        P(BOTH),
        P(BOTH),
        P(BOTH),
        P(BOTH),
        P(BOTH),
        P(BOTH),
        P(BOTH),
        P(BOTH),
    )
    out_specs = (
        P(BOTH, None),
        P(BOTH, None),
        P(BOTH, None),
        P(BOTH, None),
        P(BOTH, None),
        P(BOTH, None),
        P(BOTH, None),
        P(None, BOTH),
        P(BOTH),
        P(BOTH),
        P(BOTH),
        P(BOTH),
        P(BOTH),
        P(BOTH),
        P(BOTH),
        P(BOTH),
        P(BOTH),
    )
    return jax.shard_map(
        body, mesh=mesh, in_specs=in_specs, out_specs=out_specs, check_vma=False
    )
```

profile of v0, /device:TPU:0, one launch (start us, length us, event | category | flops | bytes accessed | tf_op | source)
XLA Modules:
  0.0 229.2 jit_solution(1664814864950418601)
XLA Ops:
  0.7 223.2 %layer.1 = (bf16[512,1024]{1,0:T(8,128)(2,1)}, f32[512,1024]{1,0:T(8,128)}, f32[32,1024]{1,0:T(8,128)}, f32[32,1024]{1,0:T(8,128)}, f32[32,1024]{1,0:T(8,128)}, ...) custom-call(bf16[512,1024]{1,0:T(8,128)(2,1)} %refs_0_.1, ...), custom_call_target="tpu_custom_call" | custom-call | tf_op jit(solution)/shard_map/layer/pallas_call | solution.py:1196
  223.9 5.1 %results.1 = (bf16[512,1024]{1,0:T(8,128)(2,1)}, f32[512,1024]{1,0:T(8,128)}, f32[32,1024]{1,0:T(8,128)}, f32[32,1024]{1,0:T(8,128)}, f32[32,1024]{1,0:T(8,128)}...) custom-call(bf16[512,1024]{1,0:T(8,128)(2,1)} %get-tuple-element.44., ...), custom_call_target="tpu_custom_call" | custom-call | tf_op jit(solution)/shard_map/results/pallas_call | solution.py:1239
where the time goes:
time: 229 us
  Pallas kernels  228 us (100%)
    pallas_call x1, Pallas kernels, layer_call(): pl.pallas_call(functools.partial(layer_kernel, depth), out_shape=tuple((j...  223 us
    pallas_call x1, Pallas kernels, results_call(): pl.pallas_call(functools.partial(results_kernel, len(large), short), out_...  5.12 us

commit v1 on v0

--- a/solution.py
+++ b/solution.py
@@ -214,8 +214,8 @@
                     self.move(name).wait_send()
 
 
-GATHER_LAGS = (0, 1, 3, 6, 6, 7, 8, 8, 9, 11)
-GATHER_ORDER = (4, 3, 5, 1, 0, 2, 6, 8, 7, 9)
+GATHER_LAGS = (0, 1, 3, 5, 5, 7, 8, 8, 9, 11)
+GATHER_ORDER = (0, 2, 5, 6, 4, 7, 1, 3, 8, 9)
 
 
 HEAD = 64
@@ -663,17 +663,17 @@
 
 SUM_SENDS = numbered("c", "df", "dg", "da", "db", "xn", "yn", "xf", "yf", "f", "m", "n")
 SUM_LAGS = (0, 1, 2, 3, 4, 3, 5, 6, 7)
-SUM_ORDER = (1, 6, 4, 2, 7, 3, 0, 5, 8)
+SUM_ORDER = (6, 1, 2, 3, 4, 5, 7, 8, 0)
 SUM_BUFFERS = {
     "grad": (2, (4, 2, 2, 2)),
     "held": (7, (4, 2, 2)),
     "c": (2, (4, 2, 2)),
     "df": (7, (2,)),
     "dg": (4, (2,)),
-    "da": (2, ()),
-    "db": (2, ()),
-    "xn": (4, (2,)),
-    "yn": (3, (2,)),
+    "da": (4, ()),
+    "db": (4, ()),
+    "xn": (5, (2,)),
+    "yn": (4, (2,)),
     "xf": (5, (2,)),
     "yf": (5, (2,)),
     "f": (5, (2,)),
@@ -902,7 +902,8 @@
     turned = jnp.transpose(jnp.broadcast_to(labels, (LANES, length)))
     mask[...] = jnp.where(turned[:, :1] == labels, 0.0, masked_score)
     lse[...] = jnp.where(turned >= 0.0, 1.0, 0.0)
-    for t in range(2, 10):
+    ready = GATHER_LAGS[8]
+    for t in range(2, ready + 1):
         gather_pump(t)
     spread_vectors(tiles, short, up_bias, depth)
     loads[BLOCKS].wait()
@@ -913,13 +914,13 @@
         bias = short[pl.ds(i // 2, 1), :] * biased
         qkvc[i] = to_half(to_half(matmul(tokens[...], square(full, i)[...]) + bias).astype(f32) * scale)
 
-    stepwise(project, [lambda: gather_pump(10), lambda: gather_pump(11), nothing])
+    stepwise(project, [lambda: gather_pump(ready + 1), lambda: gather_pump(ready + 2), nothing])
     stepwise(
         lambda i: attend_pairs(i * 4, i * 4 + 4, qkvc, lse, mask),
-        [lambda: gather_pump(12), nothing],
+        [lambda: gather_pump(ready + 3), nothing],
     )
     lse_turned[...] = jnp.transpose(lse[...])[: lse_turned.shape[0]]
-    gather_pump(13)
+    gather_pump(ready + 4)
 
     wo_full = square(full, 3)
 
@@ -959,10 +960,10 @@
     def contract(j):
         total[...] = total[...] + matmul_nt(act[j], square(full, 2 * ATTN + j)[...])
 
-    gather_pump(14)
-    stepwise(activate, [lambda: gather_pump(15), lambda: gather_pump(16), lambda: gather_pump(17), nothing])
+    gather_pump(ready + 5)
+    stepwise(activate, [lambda: gather_pump(ready + 6), lambda: gather_pump(ready + 7), lambda: gather_pump(ready + 8), nothing])
     total[...] = mid[...].astype(f32) + short[3:4, :]
-    stepwise(contract, [lambda: gather_pump(18), lambda: gather_pump(19), lambda: gather_pump(20), nothing])
+    stepwise(contract, [lambda: gather_pump(ready + 9), lambda: gather_pump(ready + 10), lambda: gather_pump(ready + 11), nothing])
 
     loads[BLOCKS + 1].wait()
     vgrads[...] = jnp.zeros_like(vgrads)
@@ -1034,7 +1035,7 @@
     turn_a[...] = jnp.transpose(half[...])
     weight_grad(0, turn_a, act.at[0])
     pump(0)
-    for t in range(21, BLOCKS + max(GATHER_LAGS)):
+    for t in range(ready + 12, BLOCKS + max(GATHER_LAGS)):
         gather_pump(t)
 
     up_grads = up_bias
@@ -1127,12 +1128,12 @@
                     )
                 )
 
-    def last_pump():
+    def middle_pump():
+        pump(9)
         place_vectors()
-        pump(11)
 
     stepwise(
-        lambda i: weight_grad(9 + i, turn_b, act.at[2 - i]), [lambda: pump(9), lambda: pump(10), last_pump]
+        lambda i: weight_grad(9 + i, turn_b, act.at[2 - i]), [middle_pump, lambda: pump(10), lambda: pump(11)]
     )
 
     def hand_back():

time: 229 us -> 219 us (0.956)
  Pallas kernels: 228 us -> 218 us
    pallas_call x1, Pallas kernels: 223 us -> 213 us  [layer_call(): pl.pallas_call(functools.partial(layer_kernel, depth), out_shape=tuple((j...]
where the time goes in v1:
time: 219 us
  Pallas kernels  218 us (100%)
    pallas_call x1, Pallas kernels, layer_call(): pl.pallas_call(functools.partial(layer_kernel, depth), out_shape=tuple((j...  213 us
    pallas_call x1, Pallas kernels, results_call(): pl.pallas_call(functools.partial(results_kernel, len(large), short), out_...  5.12 us

profile of v1, /device:TPU:0, one launch (start us, length us, event | category | flops | bytes accessed | tf_op | source)
XLA Modules:
  0.0 219.0 jit_solution(2590213754734056480)
XLA Ops:
  0.7 213.0 %layer.1 = (bf16[512,1024]{1,0:T(8,128)(2,1)}, f32[512,1024]{1,0:T(8,128)}, f32[32,1024]{1,0:T(8,128)}, f32[32,1024]{1,0:T(8,128)}, f32[32,1024]{1,0:T(8,128)}, ...) custom-call(bf16[512,1024]{1,0:T(8,128)(2,1)} %refs_0_.1, ...), custom_call_target="tpu_custom_call" | custom-call | tf_op jit(solution)/shard_map/layer/pallas_call | solution.py:1197
  213.7 5.1 %results.1 = (bf16[512,1024]{1,0:T(8,128)(2,1)}, f32[512,1024]{1,0:T(8,128)}, f32[32,1024]{1,0:T(8,128)}, f32[32,1024]{1,0:T(8,128)}, f32[32,1024]{1,0:T(8,128)}...) custom-call(bf16[512,1024]{1,0:T(8,128)(2,1)} %get-tuple-element.44., ...), custom_call_target="tpu_custom_call" | custom-call | tf_op jit(solution)/shard_map/results/pallas_call | solution.py:1240

commit v2 on v1

--- a/solution.py
+++ b/solution.py
@@ -585,6 +585,7 @@
 
 
 ATTN = 4
+NORM_ROWS = 256
 LANES = 128
 SIDE = 1024
 V_LANE, R_LANE = 32, 64
@@ -663,13 +664,13 @@
 
 SUM_SENDS = numbered("c", "df", "dg", "da", "db", "xn", "yn", "xf", "yf", "f", "m", "n")
 SUM_LAGS = (0, 1, 2, 3, 4, 3, 5, 6, 7)
-SUM_ORDER = (6, 1, 2, 3, 4, 5, 7, 8, 0)
+SUM_ORDER = (6, 3, 1, 2, 4, 5, 0, 7, 8)
 SUM_BUFFERS = {
     "grad": (2, (4, 2, 2, 2)),
     "held": (7, (4, 2, 2)),
     "c": (2, (4, 2, 2)),
     "df": (7, (2,)),
-    "dg": (4, (2,)),
+    "dg": (2, (2,)),
     "da": (4, ()),
     "db": (4, ()),
     "xn": (5, (2,)),
@@ -884,7 +885,7 @@
         return to_half(total[b * rows : (b + 1) * rows, :])
 
     def gather_block(b):
-        return GatherBlock(here, full.at[b], lambda: own(b), ss.at[b], rs.at[b], b < 2)
+        return GatherBlock(here, full.at[b], lambda: own(b), ss.at[b], rs.at[b], b < 6)
 
     own_tiles = GatherBlock(here, tiles, lambda: to_half(mine_vec[...]), ss.at[BLOCKS], rs.at[BLOCKS])
 
@@ -932,10 +933,10 @@
 
     side_loop(width // SIDE, attended)
 
-    lane_at = lax.broadcasted_iota(jnp.int32, (LANES, LANES), 1)
+    lane_at = lax.broadcasted_iota(jnp.int32, (NORM_ROWS, LANES), 1)
 
     def first_norm(i):
-        at = aligned(i * LANES, LANES)
+        at = aligned(i * NORM_ROWS, NORM_ROWS)
         values = total[at, :]
         center = values - jnp.mean(values, axis=-1, keepdims=True)
         spread = jnp.mean(center * center, axis=-1, keepdims=True)
@@ -945,7 +946,7 @@
         lse[at, :] = jnp.where(lane_at >= R_LANE, r, lse[at, :])
         mid[at, :] = to_half(unit * short[4:5, :] + short[5:6, :])
 
-    side_loop(length // LANES, first_norm)
+    side_loop(length // NORM_ROWS, first_norm)
 
     def activate(j):
         weight = square(full, ATTN + j)
@@ -969,7 +970,7 @@
     vgrads[...] = jnp.zeros_like(vgrads)
 
     def second_norm(i):
-        at = aligned(i * LANES, LANES)
+        at = aligned(i * NORM_ROWS, NORM_ROWS)
         values = total[at, :]
         center = values - jnp.mean(values, axis=-1, keepdims=True)
         spread = jnp.mean(center * center, axis=-1, keepdims=True)
@@ -989,7 +990,7 @@
         half[at, :] = to_half(d)
         vgrads[3:4, :] = vgrads[3:4, :] + jnp.sum(to_half(d).astype(jnp.float32), axis=0, keepdims=True)
 
-    side_loop(length // LANES, second_norm)
+    side_loop(length // NORM_ROWS, second_norm)
     pltpu.make_async_copy(cotangent, out_hbm, osem.at[0]).start()
 
     outs = [gdown.at[:, i * width : (i + 1) * width] for i in range(4)]
@@ -1061,7 +1062,7 @@
 
 
     def first_norm_back(i):
-        at = aligned(i * LANES, LANES)
+        at = aligned(i * NORM_ROWS, NORM_ROWS)
         e = total[at, :]
         unit = nhat[at, :].astype(f32)
         vgrads[4:5, :] = vgrads[4:5, :] + jnp.sum(e * unit, axis=0, keepdims=True)
@@ -1075,7 +1076,7 @@
         half[at, :] = d_half
         vgrads[2:3, :] = vgrads[2:3, :] + jnp.sum(d_half.astype(f32), axis=0, keepdims=True)
 
-    side_loop(length // LANES, first_norm_back)
+    side_loop(length // NORM_ROWS, first_norm_back)
     wo_full = square(full, 3)
     delta = lse
 

time: 219 us -> 217 us (level)
    pallas_call x1, Pallas kernels: 213 us -> 211 us  [layer_call(): pl.pallas_call(functools.partial(layer_kernel, depth), out_shape=tuple((j...]
where the time goes in v2:
time: 217 us
  Pallas kernels  216 us (100%)
    pallas_call x1, Pallas kernels, layer_call(): pl.pallas_call(functools.partial(layer_kernel, depth), out_shape=tuple((j...  211 us
    pallas_call x1, Pallas kernels, results_call(): pl.pallas_call(functools.partial(results_kernel, len(large), short), out_...  5.12 us

profile of v2, /device:TPU:0, one launch (start us, length us, event | category | flops | bytes accessed | tf_op | source)
XLA Modules:
  0.0 216.7 jit_solution(5411518945697764908)
XLA Ops:
  0.7 210.8 %layer.1 = (bf16[512,1024]{1,0:T(8,128)(2,1)}, f32[512,1024]{1,0:T(8,128)}, f32[32,1024]{1,0:T(8,128)}, f32[32,1024]{1,0:T(8,128)}, f32[32,1024]{1,0:T(8,128)}, ...) custom-call(bf16[512,1024]{1,0:T(8,128)(2,1)} %refs_0_.1, ...), custom_call_target="tpu_custom_call" | custom-call | tf_op jit(solution)/shard_map/layer/pallas_call | solution.py:1198
  211.4 5.1 %results.1 = (bf16[512,1024]{1,0:T(8,128)(2,1)}, f32[512,1024]{1,0:T(8,128)}, f32[32,1024]{1,0:T(8,128)}, f32[32,1024]{1,0:T(8,128)}, f32[32,1024]{1,0:T(8,128)}...) custom-call(bf16[512,1024]{1,0:T(8,128)(2,1)} %get-tuple-element.44., ...), custom_call_target="tpu_custom_call" | custom-call | tf_op jit(solution)/shard_map/results/pallas_call | solution.py:1241

commit v3 on v2

--- a/solution.py
+++ b/solution.py
@@ -873,21 +873,23 @@
         load.start()
     greet(here)
 
-    mine_vec[...] = jnp.zeros_like(mine_vec)
-    for i in range(8):
-        mine_vec[i : i + 1, 0:rows] = vectors[i][...]
-    placed = pltpu.roll(mine_vec[...], fs * rows, 1)
-    row_at = lax.broadcasted_iota(jnp.int32, (16, LANES), 0)
-    mine_vec[...] = jnp.where(row_at == 8 + fs, jnp.broadcast_to(vectors[8][...], (16, LANES)), placed)
-
     def own(b):
         loads[b].wait()
         return to_half(total[b * rows : (b + 1) * rows, :])
 
     def gather_block(b):
-        return GatherBlock(here, full.at[b], lambda: own(b), ss.at[b], rs.at[b], b < 6)
-
-    own_tiles = GatherBlock(here, tiles, lambda: to_half(mine_vec[...]), ss.at[BLOCKS], rs.at[BLOCKS])
+        return GatherBlock(here, full.at[b], lambda: own(b), ss.at[b], rs.at[b], True)
+
+    def own_vectors():
+        mine_vec[...] = jnp.zeros_like(mine_vec)
+        for i in range(8):
+            mine_vec[i : i + 1, 0:rows] = vectors[i][...]
+        placed = pltpu.roll(mine_vec[...], fs * rows, 1)
+        row_at = lax.broadcasted_iota(jnp.int32, (16, LANES), 0)
+        mine_vec[...] = jnp.where(row_at == 8 + fs, jnp.broadcast_to(vectors[8][...], (16, LANES)), placed)
+        return to_half(mine_vec[...])
+
+    own_tiles = GatherBlock(here, tiles, own_vectors, ss.at[BLOCKS], rs.at[BLOCKS])
 
     def gather_pump(t):
         for s in GATHER_ORDER:

time: 217 us -> 217 us (level)
  no operation moved by 1% of the time
where the time goes in v3:
time: 217 us
  Pallas kernels  216 us (100%)
    pallas_call x1, Pallas kernels, layer_call(): pl.pallas_call(functools.partial(layer_kernel, depth), out_shape=tuple((j...  211 us
    pallas_call x1, Pallas kernels, results_call(): pl.pallas_call(functools.partial(results_kernel, len(large), short), out_...  5.12 us

profile of v3, /device:TPU:0, one launch (start us, length us, event | category | flops | bytes accessed | tf_op | source)
XLA Modules:
  0.0 216.6 jit_solution(2659953679272537070)
XLA Ops:
  0.7 210.6 %layer.1 = (bf16[512,1024]{1,0:T(8,128)(2,1)}, f32[512,1024]{1,0:T(8,128)}, f32[32,1024]{1,0:T(8,128)}, f32[32,1024]{1,0:T(8,128)}, f32[32,1024]{1,0:T(8,128)}, ...) custom-call(bf16[512,1024]{1,0:T(8,128)(2,1)} %refs_0_.1, ...), custom_call_target="tpu_custom_call" | custom-call | tf_op jit(solution)/shard_map/layer/pallas_call | solution.py:1200
  211.3 5.1 %results.1 = (bf16[512,1024]{1,0:T(8,128)(2,1)}, f32[512,1024]{1,0:T(8,128)}, f32[32,1024]{1,0:T(8,128)}, f32[32,1024]{1,0:T(8,128)}, f32[32,1024]{1,0:T(8,128)}...) custom-call(bf16[512,1024]{1,0:T(8,128)(2,1)} %get-tuple-element.44., ...), custom_call_target="tpu_custom_call" | custom-call | tf_op jit(solution)/shard_map/results/pallas_call | solution.py:1243
